TPU v7x, 32 devices: a whole 2x2x4 slice. The times are simulated.
32 devices in a mesh: row: 8 (over z, x), col: 4 (over y, core).
Axes of the slice: x: 2, y: 2, z: 4, core: 2. Of those that a mesh axis runs over, the one named last changes fastest.
Arguments:
- features: bfloat16 [4, 1024, 256], P('col', 'row'), may hold values from -6 to 6
- weight: bfloat16 [256, 256], replicated, may hold values from -0.375 to 0.375
- tile_values: bfloat16 [8, 4, 32, 128, 128], P('row', 'col'), may hold values from -0.125 to 0.125
- tile_slots: int32 [8, 4, 32], P('row', 'col'), may hold values from 0 to 31, as said below
- tile_counts: int32 [8, 4], P('row', 'col'), may hold values from 1 to 32, as said below
- cotangent: bfloat16 [8, 512, 256], P('row', 'col'), may hold values from -6 to 6
Outputs:
- layer_out: bfloat16 [8, 512, 256], P('row', 'col')
- feature_grad: bfloat16 [4, 1024, 256], P('col', 'row')
- weight_grad: float32 [256, 256], replicated
Inputs may be any that keep to these rules, and one draw needn't show every extreme that they name: `tile_slots`: within one grid block the 32 slot positions are distinct; slots from tile_counts on carry no edges. `tile_counts`: some grid block uses all 32 slots.
All inputs are finite; a program needn't handle non-finite values.
Results may differ from a plain program's by a relative error of at most 0.022.
Values may be sent and summed in bfloat16 or wider, within the bound.
No kernel may reach another device: no remote copies, remote signals or barrier semaphores. Data moves between devices by JAX's collectives and lax.ppermute only.
A program may use at most 64 MiB of HBM per device.

v0:
```python
import math

import jax
import jax.numpy as jnp
from jax import lax
from jax.experimental import pallas as pl
from jax.experimental.pallas import tpu as pltpu
from jax.sharding import PartitionSpec as P

F32 = jnp.float32
BF16 = jnp.bfloat16
VMEM = pl.BlockSpec(memory_space=pltpu.VMEM)
SMEM = pl.BlockSpec(memory_space=pltpu.SMEM)


def params(rows, cols):
    return pltpu.CompilerParams(vmem_limit_bytes=min(8 * 2**20 + 6 * rows * cols, 56 * 2**20))


def shape(*dims, dtype=BF16):
    return jax.ShapeDtypeStruct(dims, dtype)


def rows_of(index, slab):
    return pl.ds(pl.multiple_of(index * slab, slab), slab)


def backward_kernel(me_ref, slots_ref, count_ref, tiles_ref, *refs):
    *cot_refs, adj_ref, cot_ref, keep_ref, send_ref, total = refs
    slot_count, tile, _ = tiles_ref.shape
    half, slab, _ = keep_ref.shape
    col_tiles = adj_ref.shape[1] // tile
    adj_ref[...] = jnp.zeros_like(adj_ref)

    def place(k, carry):
        slot = slots_ref[k]
        row = pl.multiple_of((slot // col_tiles) * tile, tile)
        col = pl.multiple_of((slot % col_tiles) * tile, tile)
        adj_ref[pl.ds(row, tile), pl.ds(col, tile)] = tiles_ref[k]
        return carry

    lax.fori_loop(0, jnp.minimum(count_ref[0], slot_count), place, 0)
    for k, ref in enumerate(cot_refs):
        cot_ref[rows_of(me_ref[1] ^ k, slab), :] = ref[...]
    total[...] = lax.dot_general(
        adj_ref[...], cot_ref[...], (((0,), (0,)), ((), ())), preferred_element_type=F32
    ).astype(BF16)
    side = me_ref[0] & 1
    for m in range(half):
        keep_ref[m] = total[rows_of(2 * m + side, slab), :]
        send_ref[m] = total[rows_of(2 * m + 1 - side, slab), :]


def pair_sum_kernel(me_ref, keep_ref, got_ref, *chunk_refs):
    for k, ref in enumerate(chunk_refs):
        m = (me_ref[0] >> 1) ^ k
        ref[...] = (keep_ref[m].astype(F32) + got_ref[m].astype(F32)).astype(BF16)


def forward_kernel(me_ref, adj_ref, column_ref, cot_ref, *refs):
    *chunk_refs, grad_ref, total = refs
    slab = chunk_refs[0].shape[0]
    part = jnp.dot(adj_ref[...], column_ref[...], preferred_element_type=F32).astype(BF16)
    total[...] = part
    grad_ref[...] = lax.dot_general(
        part, cot_ref[...], (((0,), (0,)), ((), ())), preferred_element_type=F32
    ).astype(BF16)
    for k, ref in enumerate(chunk_refs):
        ref[...] = total[rows_of(me_ref[1] ^ k, slab), :]


def grad_sum_kernel(terms_ref, *refs, scale):
    out_ref = refs[-1]
    total = jnp.sum(terms_ref[...].astype(F32), axis=0) * scale
    out_ref[...] = jnp.broadcast_to(total.astype(BF16)[None], out_ref.shape)


def product_kernel(weight_ref, *refs, contract):
    *term_refs, out_ref = refs
    total = term_refs[0][...].astype(F32)
    for ref in term_refs[1:]:
        total = total + ref[...].astype(F32)
    out_ref[...] = lax.dot_general(
        total.astype(BF16),
        weight_ref[...],
        (((1,), (contract,)), ((), ())),
        preferred_element_type=F32,
    ).astype(BF16)


def summed_product(weight, terms, contract, name, compiler_params):
    return pl.pallas_call(
        lambda *refs: product_kernel(*refs, contract=contract),
        out_shape=shape(*terms[0].shape),
        in_specs=[VMEM] * (1 + len(terms)),
        out_specs=VMEM,
        compiler_params=compiler_params,
        name=name,
    )(weight, *terms)


def swap(array, axis, distance):
    pairs = [(i, i ^ distance) for i in range(lax.axis_size(axis))]
    return lax.ppermute(array, axis, pairs)


def exchange(chunks, axis, stride=1):
    return [chunks[0]] + [swap(chunks[k], axis, k * stride) for k in range(1, len(chunks))]


def body(features, weight, tile_values, tile_slots, tile_counts, cotangent):
    row_devices = lax.axis_size("row")
    col_devices = lax.axis_size("col")
    devices = row_devices * col_devices
    slab, width = features.shape[1:]
    rows, cols = col_devices * slab, row_devices * slab
    limits = params(rows, cols)
    me = jnp.stack([lax.axis_index("row"), lax.axis_index("col")]).astype(jnp.int32)

    column = lax.all_to_all(
        jnp.broadcast_to(features, (row_devices, slab, width)), "row", 0, 0, tiled=True
    ).reshape(cols, width)
    cots = exchange([cotangent[0]] * col_devices, "col")

    half = row_devices // 2
    adj, cot_block, keep, send = pl.pallas_call(
        backward_kernel,
        out_shape=[shape(rows, cols), shape(rows, width)] + [shape(half, slab, width)] * 2,
        in_specs=[SMEM] * 3 + [VMEM] * (1 + col_devices),
        out_specs=[VMEM] * 4,
        scratch_shapes=[pltpu.VMEM((cols, width), BF16)],
        compiler_params=limits,
        name="backward",
    )(me, tile_slots[0, 0], tile_counts[0], tile_values[0, 0], *cots)
    column_chunks = pl.pallas_call(
        pair_sum_kernel,
        out_shape=[shape(slab, width)] * half,
        in_specs=[SMEM, VMEM, VMEM],
        out_specs=[VMEM] * half,
        compiler_params=limits,
        name="pair_sum",
    )(me, keep, swap(send, "row", 1))
    column_terms = exchange(column_chunks, "row", 2)

    *row_chunks, grad = pl.pallas_call(
        forward_kernel,
        out_shape=[shape(slab, width)] * col_devices + [shape(width, width)],
        in_specs=[SMEM] + [VMEM] * 3,
        out_specs=[VMEM] * (col_devices + 1),
        scratch_shapes=[pltpu.VMEM((rows, width), BF16)],
        compiler_params=limits,
        name="forward",
    )(me, adj, column, cot_block)
    row_terms = exchange(row_chunks, "col")

    chunk_shape = (
        (width // devices, width) if width % devices == 0 else (1, width * width // devices)
    )
    grad_terms = lax.all_to_all(
        grad.reshape(devices, *chunk_shape), ("row", "col"), 0, 0, tiled=True
    )
    scale = 1.0 / math.sqrt(devices * slab)
    grad_chunks = pl.pallas_call(
        lambda *refs: grad_sum_kernel(*refs, scale=scale),
        out_shape=shape(devices, *chunk_shape),
        in_specs=[VMEM] + [pl.BlockSpec(memory_space=pl.ANY)] * half,
        out_specs=VMEM,
        compiler_params=limits,
        name="grad_sum",
    )(grad_terms, *column_chunks)
    grad_all = lax.all_to_all(grad_chunks, ("row", "col"), 0, 0, tiled=True)
    weight_grad = grad_all.astype(F32).reshape(width, width)

    layer_out = summed_product(weight, row_terms, 0, "layer_out", limits)
    feature_grad = summed_product(weight, column_terms, 1, "feature_grad", limits)
    return (layer_out[None], feature_grad[None], weight_grad)


def solution(mesh):
    placed = (
        P("col", "row", None),
        P(),
        P("row", "col", None, None, None),
        P("row", "col", None),
        P("row", "col"),
        P("row", "col", None),
    )
    return jax.shard_map(
        body,
        mesh=mesh,
        in_specs=placed,
        out_specs=(P("row", "col", None), P("col", "row", None), P()),
        check_vma=False,
    )
```

profile of v0, /device:TPU:0, one launch (start us, length us, event | category | flops | bytes accessed | tf_op | source)
XLA Modules:
  0.0 55.0 jit_solution(13859203330703063511)
XLA Ops:
  0.6 0.0 copy-start
  0.6 1.8 %broadcast_in_dim.14 = bf16[8,128,256]{2,1,0:T(8,128)(2,1)} broadcast(bf16[128,256]{1,0:T(8,128)(2,1)} %bitcast.22), dimensions={1,2} | broadcast | bytes 589824 | tf_op jit(solution)/shard_map/broadcast_in_dim | solution.py:121
  2.4 0.0 copy-start.2
  2.4 7.4 %all-to-all-start = ((bf16[8,128,256]{2,1,0:T(8,128)(2,1)}), bf16[8,128,256]{2,1,0:T(8,128)(2,1)S(1)}, u32[]{:S(2)}, u32[]{:S(2)}) async-start(bf16[8,128,256]{2,1,0:T(8,128)(2,1)} %broadcast_in_dim.14), calls=%async_computation | async-start | bytes 1048576 | tf_op jit(solution)/shard_map/all_to_all | solution.py:120
  9.8 0.0 copy-done.2
  9.8 0.1 collective-permute-start
  9.9 1.6 %collective-permute-start.1 = (bf16[128,256]{1,0:T(8,128)(2,1)S(1)}, bf16[128,256]{1,0:T(8,128)(2,1)S(1)}, u32[]{:S(2)}, u32[]{:S(2)}) collective-permute-start(bf16[128,256]{1,0:T(8,128)(2,1)S(1)} %bitcast.18), channel_id=1, source_target_pairs={{0,2},{1,3},{2,0},{3,1},{4,6},{5,7},{6,4},{7,5},{8,10},{9,11},{10,... | collective-permute-start | bytes 196616 | tf_op jit(solution)/shard_map/ppermute | solution.py:104
  11.5 0.3 collective-permute-start.2
  12.4 0.1 pad_add_fusion.me_ref
  12.5 0.0 collective-permute-done.refs_1_
  12.5 1.9 %collective-permute-done.1.refs_2_ = bf16[128,256]{1,0:T(8,128)(2,1)S(1)} collective-permute-done((bf16[128,256]{1,0:T(8,128)(2,1)S(1)}, bf16[128,256]{1,0:T(8,128)(2,1)S(1)}, u32[]{:S(2)}, u32[]{:S(2)}) %collective-permute-start.1) | collective-permute-done | bytes 65568 | tf_op jit(solution)/shard_map/ppermute | solution.py:104
  14.4 1.1 %collective-permute-done.2.refs_3_ = bf16[128,256]{1,0:T(8,128)(2,1)S(1)} collective-permute-done((bf16[128,256]{1,0:T(8,128)(2,1)S(1)}, bf16[128,256]{1,0:T(8,128)(2,1)S(1)}, u32[]{:S(2)}, u32[]{:S(2)}) %collective-permute-start.2) | collective-permute-done | bytes 65568 | tf_op jit(solution)/shard_map/ppermute | solution.py:104
  15.5 0.0 copy-start.3
  15.5 0.0 copy-done
  15.5 0.7 %copy-done.3 = s32[1,1,32]{2,1,0:T(1,128)S(1)} copy-done((s32[1,1,32]{2,1,0:T(1,128)S(1)}, s32[1,1,32]{2,1,0:T(1,128)}, u32[]{:S(2)}) %copy-start.3) | copy-done | bytes 152
  16.2 2.1 %backward.1 = (bf16[512,1024]{1,0:T(8,128)(2,1)S(1)}, bf16[512,256]{1,0:T(8,128)(2,1)S(1)}, bf16[4,128,256]{2,1,0:T(8,128)(2,1)S(1)}, bf16[4,128,256]{2,1,0:T(8,128)(2,1)}) custom-call(s32[2]{0:T(128)S(1)} %pad_add_fusion.me_ref, s32[32]{0:T(128)S(1)} %bitcast.21, s32[1]{0:T(128)} %bitcast.14.count_ref, bf16[32,128,128]{2,1,0:T(8,128)(2,1)S(1)} %bitcast.16, ...), custom_call_target="tpu_custom_call" | custom-call | tf_op jit(solution)/shard_map/backward/pallas_call | solution.py:126
  18.3 1.8 %collective-permute-start.6 = (bf16[4,128,256]{2,1,0:T(8,128)(2,1)}, bf16[4,128,256]{2,1,0:T(8,128)(2,1)S(1)}, u32[]{:S(2)}, u32[]{:S(2)}) collective-permute-start(bf16[4,128,256]{2,1,0:T(8,128)(2,1)} %get-tuple-element.23), channel_id=1, source_target_pairs={{0,4},{4,0},{8,12},{12,8},{16,20},{20,16},{24,28},{28,24},{1,5},{5... | collective-permute-start | bytes 786440 | tf_op jit(solution)/shard_map/ppermute | solution.py:104
  20.1 4.2 %all-to-all-done = bf16[8,128,256]{2,1,0:T(8,128)(2,1)S(1)} async-done(((bf16[8,128,256]{2,1,0:T(8,128)(2,1)}), bf16[8,128,256]{2,1,0:T(8,128)(2,1)S(1)}, u32[]{:S(2)}, u32[]{:S(2)}) %all-to-all-start) | async-done | bytes 524320 | tf_op jit(solution)/shard_map/all_to_all | solution.py:120
  24.3 1.9 %forward.1 = (bf16[128,256]{1,0:T(8,128)(2,1)S(1)}, bf16[128,256]{1,0:T(8,128)(2,1)S(1)}, bf16[128,256]{1,0:T(8,128)(2,1)S(1)}, bf16[128,256]{1,0:T(8,128)(2,1)S(1)}, bf16[256,256]{1,0:T(8,128)(2,1)}) custom-call(s32[2]{0:T(128)S(1)} %pad_add_fusion.me_ref, bf16[512,1024]{1,0:T(8,128)(2,1)S(1)} %get-tuple-element.16.adj_ref, bf16[1024,256]{1,0:T(8,128)(2,1)S(1)} %bitcast.15, ...), custom_call_target="tpu_custom_call" | custom-call | tf_op jit(solution)/shard_map/forward/pallas_call | solution.py:145
  26.2 3.7 %all-to-all-start.1 = ((bf16[32,8,256]{2,1,0:T(8,128)(2,1)}), bf16[32,8,256]{2,1,0:T(8,128)(2,1)S(1)}, u32[]{:S(2)}, u32[]{:S(2)}) async-start(bf16[32,8,256]{2,1,0:T(8,128)(2,1)} %bitcast.10), calls=%async_computation.1 | async-start | bytes 262144 | tf_op jit(solution)/shard_map/all_to_all | solution.py:159
  29.9 0.0 collective-permute-done.6.got_ref
  29.9 0.6 %pair_sum.1 = (bf16[128,256]{1,0:T(8,128)(2,1)S(1)}, bf16[128,256]{1,0:T(8,128)(2,1)S(1)}, bf16[128,256]{1,0:T(8,128)(2,1)S(1)}, bf16[128,256]{1,0:T(8,128)(2,1)S(1)}) custom-call(s32[2]{0:T(128)S(1)} %pad_add_fusion.me_ref, bf16[4,128,256]{2,1,0:T(8,128)(2,1)S(1)} %get-tuple-element.22.keep_ref, bf16[4,128,256]{2,1,0:T(8,128)(2,1)S(1)} %collective-permute-done.6.got_ref), custom_call_target="tpu_custom_call" | custom-call | tf_op jit(solution)/shard_map/pair_sum/pallas_call | solution.py:135
  30.5 7.6 %all-to-all-done.1.refs_0_ = bf16[32,8,256]{2,1,0:T(8,128)(2,1)S(1)} async-done(((bf16[32,8,256]{2,1,0:T(8,128)(2,1)}), bf16[32,8,256]{2,1,0:T(8,128)(2,1)S(1)}, u32[]{:S(2)}, u32[]{:S(2)}) %all-to-all-start.1) | async-done | bytes 131104 | tf_op jit(solution)/shard_map/all_to_all | solution.py:159
  38.1 0.7 %grad_sum.1 = bf16[32,8,256]{2,1,0:T(8,128)(2,1)} custom-call(bf16[32,8,256]{2,1,0:T(8,128)(2,1)S(1)} %all-to-all-done.1.refs_0_, bf16[128,256]{1,0:T(8,128)(2,1)S(1)} %get-tuple-element.24.refs_1_, bf16[128,256]{1,0:T(8,128)(2,1)S(1)} %get-tuple-element.25.refs_2_, bf16[128,256]{1,0:T(8,128)(2,1)S(1)} %get-tuple-element.26.refs_3_, ...), custom_call_target="tpu_custom_call" | custom-call | tf_op jit(solution)/shard_map/grad_sum/pallas_call | solution.py:163
  38.8 0.0 copy-start.1
  38.8 2.7 %all-to-all-start.2 = ((bf16[32,8,256]{2,1,0:T(8,128)(2,1)}), bf16[32,8,256]{2,1,0:T(8,128)(2,1)S(1)}, u32[]{:S(2)}, u32[]{:S(2)}) async-start(bf16[32,8,256]{2,1,0:T(8,128)(2,1)} %grad_sum.1), calls=%async_computation.2 | async-start | bytes 262144 | tf_op jit(solution)/shard_map/all_to_all | solution.py:171
  41.5 1.8 %collective-permute-start.7 = (bf16[128,256]{1,0:T(8,128)(2,1)S(1)}, bf16[128,256]{1,0:T(8,128)(2,1)S(1)}, u32[]{:S(2)}, u32[]{:S(2)}) collective-permute-start(bf16[128,256]{1,0:T(8,128)(2,1)S(1)} %get-tuple-element.25.refs_2_), channel_id=1, source_target_pairs={{0,8},{4,12},{8,0},{12,4},{16,24},{20,28},{24,16},{28,20},{1,9},{5... | collective-permute-start | bytes 196616 | tf_op jit(solution)/shard_map/ppermute | solution.py:104
  43.3 2.5 %collective-permute-start.8 = (bf16[128,256]{1,0:T(8,128)(2,1)S(1)}, bf16[128,256]{1,0:T(8,128)(2,1)S(1)}, u32[]{:S(2)}, u32[]{:S(2)}) collective-permute-start(bf16[128,256]{1,0:T(8,128)(2,1)S(1)} %get-tuple-element.26.refs_3_), channel_id=1, source_target_pairs={{0,16},{4,20},{8,24},{12,28},{16,0},{20,4},{24,8},{28,12},{1,17},{... | collective-permute-start | bytes 196616 | tf_op jit(solution)/shard_map/ppermute | solution.py:104
  45.8 0.2 collective-permute-start.9
  46.0 0.0 collective-permute-start.3
  46.0 1.7 %collective-permute-start.4 = (bf16[128,256]{1,0:T(8,128)(2,1)S(1)}, bf16[128,256]{1,0:T(8,128)(2,1)S(1)}, u32[]{:S(2)}, u32[]{:S(2)}) collective-permute-start(bf16[128,256]{1,0:T(8,128)(2,1)S(1)} %get-tuple-element.20), channel_id=1, source_target_pairs={{0,2},{1,3},{2,0},{3,1},{4,6},{5,7},{6,4},{7,5},{8,10},{9,11},{10,... | collective-permute-start | bytes 196616 | tf_op jit(solution)/shard_map/ppermute | solution.py:104
  47.6 0.1 collective-permute-done.7.refs_2_
  47.8 0.1 collective-permute-start.5
  47.8 2.4 %collective-permute-done.8.refs_3_ = bf16[128,256]{1,0:T(8,128)(2,1)S(1)} collective-permute-done((bf16[128,256]{1,0:T(8,128)(2,1)S(1)}, bf16[128,256]{1,0:T(8,128)(2,1)S(1)}, u32[]{:S(2)}, u32[]{:S(2)}) %collective-permute-start.8) | collective-permute-done | bytes 65568 | tf_op jit(solution)/shard_map/ppermute | solution.py:104
  50.3 2.4 %collective-permute-done.9.refs_4_ = bf16[128,256]{1,0:T(8,128)(2,1)S(1)} collective-permute-done((bf16[128,256]{1,0:T(8,128)(2,1)S(1)}, bf16[128,256]{1,0:T(8,128)(2,1)S(1)}, u32[]{:S(2)}, u32[]{:S(2)}) %collective-permute-start.9) | collective-permute-done | bytes 65568 | tf_op jit(solution)/shard_map/ppermute | solution.py:104
  52.7 0.0 copy-done.1
  52.7 0.8 %feature_grad.1 = bf16[128,256]{1,0:T(8,128)(2,1)} custom-call(bf16[256,256]{1,0:T(8,128)(2,1)S(1)} %copy-done.1, bf16[128,256]{1,0:T(8,128)(2,1)S(1)} %get-tuple-element.24.refs_1_, bf16[128,256]{1,0:T(8,128)(2,1)S(1)} %collective-permute-done.7.refs_2_, bf16[128,256]{1,0:T(8,128)(2,1)S(1)} %collective-permute-done.8.refs_3_, ...), custom_call_target="tpu_custom_call" | custom-call | tf_op jit(solution)/shard_map/feature_grad/pallas_call | solution.py:92
  53.5 0.0 collective-permute-done.3.refs_2_
  53.5 0.0 collective-permute-done.4.refs_3_
  53.5 0.0 collective-permute-done.5.refs_4_
  53.5 0.8 %layer_out.1 = bf16[128,256]{1,0:T(8,128)(2,1)} custom-call(bf16[256,256]{1,0:T(8,128)(2,1)S(1)} %copy-done.1, bf16[128,256]{1,0:T(8,128)(2,1)S(1)} %get-tuple-element.18.refs_1_, bf16[128,256]{1,0:T(8,128)(2,1)S(1)} %collective-permute-done.3.refs_2_, bf16[128,256]{1,0:T(8,128)(2,1)S(1)} %collective-permute-done.4.refs_3_, ...), custom_call_target="tpu_custom_call" | custom-call | tf_op jit(solution)/shard_map/layer_out/pallas_call | solution.py:92
  54.3 0.0 all-to-all-done.2
  54.3 0.7 %bitcast_convert_fusion = f32[256,256]{1,0:T(8,128)} fusion(bf16[32,8,256]{2,1,0:T(8,128)(2,1)S(1)} %all-to-all-done.2), kind=kLoop, calls=%fused_computation | loop fusion | flops 65536 | bytes 393216 | tf_op jit(solution)/shard_map/reshape | solution.py:172
Async XLA Ops:
  0.6 14.9 %copy-start = (bf16[1,1,32,128,128]{4,3,2,1,0:T(8,128)(2,1)S(1)}, bf16[1,1,32,128,128]{4,3,2,1,0:T(8,128)(2,1)}, u32[]{:S(2)}) copy-start(bf16[1,1,32,128,128]{4,3,2,1,0:T(8,128)(2,1)} %param.8) | copy-start | bytes 3145732
  2.4 7.4 %copy-start.2 = (bf16[1,128,256]{2,1,0:T(8,128)(2,1)S(1)}, bf16[1,128,256]{2,1,0:T(8,128)(2,1)}, u32[]{:S(2)}) copy-start(bf16[1,128,256]{2,1,0:T(8,128)(2,1)} %param.11) | copy-start | bytes 196612
  2.4 21.9 %all-to-all-start = ((bf16[8,128,256]{2,1,0:T(8,128)(2,1)}), bf16[8,128,256]{2,1,0:T(8,128)(2,1)S(1)}, u32[]{:S(2)}, u32[]{:S(2)}) async-start(bf16[8,128,256]{2,1,0:T(8,128)(2,1)} %broadcast_in_dim.14), calls=%async_computation | async-start | bytes 1048576 | tf_op jit(solution)/shard_map/all_to_all | solution.py:120
  9.8 2.7 %collective-permute-start = (bf16[128,256]{1,0:T(8,128)(2,1)S(1)}, bf16[128,256]{1,0:T(8,128)(2,1)S(1)}, u32[]{:S(2)}, u32[]{:S(2)}) collective-permute-start(bf16[128,256]{1,0:T(8,128)(2,1)S(1)} %bitcast.17), channel_id=1, source_target_pairs={{0,1},{1,0},{2,3},{3,2},{4,5},{5,4},{6,7},{7,6},{8,9},{9,8},{10,11... | collective-permute-start | bytes 196616 | tf_op jit(solution)/shard_map/ppermute | solution.py:104
  9.9 4.5 %collective-permute-start.1 = (bf16[128,256]{1,0:T(8,128)(2,1)S(1)}, bf16[128,256]{1,0:T(8,128)(2,1)S(1)}, u32[]{:S(2)}, u32[]{:S(2)}) collective-permute-start(bf16[128,256]{1,0:T(8,128)(2,1)S(1)} %bitcast.18), channel_id=1, source_target_pairs={{0,2},{1,3},{2,0},{3,1},{4,6},{5,7},{6,4},{7,5},{8,10},{9,11},{10,... | collective-permute-start | bytes 196616 | tf_op jit(solution)/shard_map/ppermute | solution.py:104
  11.5 4.0 %collective-permute-start.2 = (bf16[128,256]{1,0:T(8,128)(2,1)S(1)}, bf16[128,256]{1,0:T(8,128)(2,1)S(1)}, u32[]{:S(2)}, u32[]{:S(2)}) collective-permute-start(bf16[128,256]{1,0:T(8,128)(2,1)S(1)} %bitcast.19), channel_id=1, source_target_pairs={{0,3},{1,2},{2,1},{3,0},{4,7},{5,6},{6,5},{7,4},{8,11},{9,10},{10,... | collective-permute-start | bytes 196616 | tf_op jit(solution)/shard_map/ppermute | solution.py:104
  15.5 0.7 %copy-start.3 = (s32[1,1,32]{2,1,0:T(1,128)S(1)}, s32[1,1,32]{2,1,0:T(1,128)}, u32[]{:S(2)}) copy-start(s32[1,1,32]{2,1,0:T(1,128)} %param.9) | copy-start | bytes 388
  18.3 11.6 %collective-permute-start.6 = (bf16[4,128,256]{2,1,0:T(8,128)(2,1)}, bf16[4,128,256]{2,1,0:T(8,128)(2,1)S(1)}, u32[]{:S(2)}, u32[]{:S(2)}) collective-permute-start(bf16[4,128,256]{2,1,0:T(8,128)(2,1)} %get-tuple-element.23), channel_id=1, source_target_pairs={{0,4},{4,0},{8,12},{12,8},{16,20},{20,16},{24,28},{28,24},{1,5},{5... | collective-permute-start | bytes 786440 | tf_op jit(solution)/shard_map/ppermute | solution.py:104
  26.2 11.9 %all-to-all-start.1 = ((bf16[32,8,256]{2,1,0:T(8,128)(2,1)}), bf16[32,8,256]{2,1,0:T(8,128)(2,1)S(1)}, u32[]{:S(2)}, u32[]{:S(2)}) async-start(bf16[32,8,256]{2,1,0:T(8,128)(2,1)} %bitcast.10), calls=%async_computation.1 | async-start | bytes 262144 | tf_op jit(solution)/shard_map/all_to_all | solution.py:159
  38.8 13.9 %copy-start.1 = (bf16[256,256]{1,0:T(8,128)(2,1)S(1)}, bf16[256,256]{1,0:T(8,128)(2,1)}, u32[]{:S(2)}) copy-start(bf16[256,256]{1,0:T(8,128)(2,1)} %refs_0_.3) | copy-start | bytes 393220
  38.8 15.5 %all-to-all-start.2 = ((bf16[32,8,256]{2,1,0:T(8,128)(2,1)}), bf16[32,8,256]{2,1,0:T(8,128)(2,1)S(1)}, u32[]{:S(2)}, u32[]{:S(2)}) async-start(bf16[32,8,256]{2,1,0:T(8,128)(2,1)} %grad_sum.1), calls=%async_computation.2 | async-start | bytes 262144 | tf_op jit(solution)/shard_map/all_to_all | solution.py:171
  41.5 6.3 %collective-permute-start.7 = (bf16[128,256]{1,0:T(8,128)(2,1)S(1)}, bf16[128,256]{1,0:T(8,128)(2,1)S(1)}, u32[]{:S(2)}, u32[]{:S(2)}) collective-permute-start(bf16[128,256]{1,0:T(8,128)(2,1)S(1)} %get-tuple-element.25.refs_2_), channel_id=1, source_target_pairs={{0,8},{4,12},{8,0},{12,4},{16,24},{20,28},{24,16},{28,20},{1,9},{5... | collective-permute-start | bytes 196616 | tf_op jit(solution)/shard_map/ppermute | solution.py:104
  43.3 7.0 %collective-permute-start.8 = (bf16[128,256]{1,0:T(8,128)(2,1)S(1)}, bf16[128,256]{1,0:T(8,128)(2,1)S(1)}, u32[]{:S(2)}, u32[]{:S(2)}) collective-permute-start(bf16[128,256]{1,0:T(8,128)(2,1)S(1)} %get-tuple-element.26.refs_3_), channel_id=1, source_target_pairs={{0,16},{4,20},{8,24},{12,28},{16,0},{20,4},{24,8},{28,12},{1,17},{... | collective-permute-start | bytes 196616 | tf_op jit(solution)/shard_map/ppermute | solution.py:104
  45.8 6.9 %collective-permute-start.9 = (bf16[128,256]{1,0:T(8,128)(2,1)S(1)}, bf16[128,256]{1,0:T(8,128)(2,1)S(1)}, u32[]{:S(2)}, u32[]{:S(2)}) collective-permute-start(bf16[128,256]{1,0:T(8,128)(2,1)S(1)} %get-tuple-element.27.refs_4_), channel_id=1, source_target_pairs={{0,24},{4,28},{8,16},{12,20},{16,8},{20,12},{24,0},{28,4},{1,25},{... | collective-permute-start | bytes 196616 | tf_op jit(solution)/shard_map/ppermute | solution.py:104
  46.0 7.5 %collective-permute-start.3 = (bf16[128,256]{1,0:T(8,128)(2,1)S(1)}, bf16[128,256]{1,0:T(8,128)(2,1)S(1)}, u32[]{:S(2)}, u32[]{:S(2)}) collective-permute-start(bf16[128,256]{1,0:T(8,128)(2,1)S(1)} %get-tuple-element.19), channel_id=1, source_target_pairs={{0,1},{1,0},{2,3},{3,2},{4,5},{5,4},{6,7},{7,6},{8,9},{9,8},{10,11... | collective-permute-start | bytes 196616 | tf_op jit(solution)/shard_map/ppermute | solution.py:104
  46.0 7.5 %collective-permute-start.4 = (bf16[128,256]{1,0:T(8,128)(2,1)S(1)}, bf16[128,256]{1,0:T(8,128)(2,1)S(1)}, u32[]{:S(2)}, u32[]{:S(2)}) collective-permute-start(bf16[128,256]{1,0:T(8,128)(2,1)S(1)} %get-tuple-element.20), channel_id=1, source_target_pairs={{0,2},{1,3},{2,0},{3,1},{4,6},{5,7},{6,4},{7,5},{8,10},{9,11},{10,... | collective-permute-start | bytes 196616 | tf_op jit(solution)/shard_map/ppermute | solution.py:104
  47.8 5.7 %collective-permute-start.5 = (bf16[128,256]{1,0:T(8,128)(2,1)S(1)}, bf16[128,256]{1,0:T(8,128)(2,1)S(1)}, u32[]{:S(2)}, u32[]{:S(2)}) collective-permute-start(bf16[128,256]{1,0:T(8,128)(2,1)S(1)} %get-tuple-element.21), channel_id=1, source_target_pairs={{0,3},{1,2},{2,1},{3,0},{4,7},{5,6},{6,5},{7,4},{8,11},{9,10},{10,... | collective-permute-start | bytes 196616 | tf_op jit(solution)/shard_map/ppermute | solution.py:104
where the time goes:
time: 55.4 us; the launch traced here: 55 us
  starting transfers between devices  23.7 us (43%)
  waiting for transfers between devices  19.8 us (36%)
  Pallas kernels  6.97 us (13%)
  local copies, waits for them, and re-layouts  2.43 us (4%)
  between operations  1.35 us (2%)
  other arithmetic  0.8 us (1%)
    ppermute x10, starting transfers between devices, swap(): return lax.ppermute(array, axis, pairs)  9.93 us
    ppermute x10, waiting for transfers between devices, swap(): return lax.ppermute(array, axis, pairs)  8.02 us
    all_to_all x1, waiting for transfers between devices, body(): lax.all_to_all(grad.reshape(devices, *chunk_shape), ('row', 'col'), 0, 0,...  7.6 us
    all_to_all x1, starting transfers between devices, body(): lax.all_to_all(jnp.broadcast_to(features, (row_devices, slab, width)), 'r...  7.38 us
    all_to_all x1, waiting for transfers between devices, body(): lax.all_to_all(jnp.broadcast_to(features, (row_devices, slab, width)), 'r...  4.16 us
    all_to_all x1, starting transfers between devices, body(): lax.all_to_all(grad.reshape(devices, *chunk_shape), ('row', 'col'), 0, 0,...  3.68 us
    all_to_all x1, starting transfers between devices, body(): grad_all = lax.all_to_all(grad_chunks, ('row', 'col'), 0, 0, tiled=True)  2.71 us
    pallas_call x1, Pallas kernels, body(): pl.pallas_call(backward_kernel, out_shape=[shape(rows, cols), shape(rows,...  2.12 us
  transfers between devices with their start and end apart: 13, of which 7 were waited for; matrix products, arithmetic and copies ran while one was open for 0% of the time, Pallas kernels for 11%

commit v1 on v0

--- a/solution.py
+++ b/solution.py
@@ -17,6 +17,12 @@
     return pltpu.CompilerParams(vmem_limit_bytes=min(8 * 2**20 + 6 * rows * cols, 56 * 2**20))
 
 
+def hint(microseconds):
+    return pl.CostEstimate(
+        flops=int(microseconds * 1e9), bytes_accessed=int(microseconds * 3.6e6), transcendentals=0
+    )
+
+
 def shape(*dims, dtype=BF16):
     return jax.ShapeDtypeStruct(dims, dtype)
 
@@ -25,10 +31,10 @@
     return pl.ds(pl.multiple_of(index * slab, slab), slab)
 
 
-def backward_kernel(me_ref, slots_ref, count_ref, tiles_ref, *refs):
-    *cot_refs, adj_ref, cot_ref, keep_ref, send_ref, total = refs
+def backward_kernel(me_ref, slots_ref, count_ref, tiles_ref, *refs, col_devices):
+    cot_refs, (adj_ref, cot_ref, *pair_refs, total) = refs[:col_devices], refs[col_devices:]
     slot_count, tile, _ = tiles_ref.shape
-    half, slab, _ = keep_ref.shape
+    half, slab = len(pair_refs), pair_refs[0].shape[1]
     col_tiles = adj_ref.shape[1] // tile
     adj_ref[...] = jnp.zeros_like(adj_ref)
 
@@ -45,28 +51,33 @@
     total[...] = lax.dot_general(
         adj_ref[...], cot_ref[...], (((0,), (0,)), ((), ())), preferred_element_type=F32
     ).astype(BF16)
-    side = me_ref[0] & 1
-    for m in range(half):
-        keep_ref[m] = total[rows_of(2 * m + side, slab), :]
-        send_ref[m] = total[rows_of(2 * m + 1 - side, slab), :]
-
-
-def pair_sum_kernel(me_ref, keep_ref, got_ref, *chunk_refs):
-    for k, ref in enumerate(chunk_refs):
-        m = (me_ref[0] >> 1) ^ k
-        ref[...] = (keep_ref[m].astype(F32) + got_ref[m].astype(F32)).astype(BF16)
-
-
-def forward_kernel(me_ref, adj_ref, column_ref, cot_ref, *refs):
-    *chunk_refs, grad_ref, total = refs
+    for k, ref in enumerate(pair_refs):
+        ref[0] = total[rows_of(me_ref[0] ^ k, slab), :]
+        ref[1] = total[rows_of(me_ref[0] ^ k ^ half, slab), :]
+
+
+def forward_kernel(me_ref, adj_ref, cot_ref, *refs, half):
+    pair_refs, (grad_ref, *chunk_refs, column, total) = refs[:half], refs[half:]
     slab = chunk_refs[0].shape[0]
-    part = jnp.dot(adj_ref[...], column_ref[...], preferred_element_type=F32).astype(BF16)
+    for k, ref in enumerate(pair_refs):
+        column[rows_of(me_ref[0] ^ k, slab), :] = ref[0]
+        column[rows_of(me_ref[0] ^ k ^ half, slab), :] = ref[1]
+    part = jnp.dot(adj_ref[...], column[...], preferred_element_type=F32).astype(BF16)
     total[...] = part
     grad_ref[...] = lax.dot_general(
         part, cot_ref[...], (((0,), (0,)), ((), ())), preferred_element_type=F32
     ).astype(BF16)
     for k, ref in enumerate(chunk_refs):
         ref[...] = total[rows_of(me_ref[1] ^ k, slab), :]
+
+
+def pair_sum_kernel(*refs):
+    *pair_refs, keep_ref, send_ref = refs
+    total = pair_refs[0][...].astype(F32)
+    for ref in pair_refs[1:]:
+        total = total + ref[...].astype(F32)
+    keep_ref[...] = total[0]
+    send_ref[...] = total[1].astype(BF16)
 
 
 def grad_sum_kernel(terms_ref, *refs, scale):
@@ -117,40 +128,41 @@
     limits = params(rows, cols)
     me = jnp.stack([lax.axis_index("row"), lax.axis_index("col")]).astype(jnp.int32)
 
-    column = lax.all_to_all(
-        jnp.broadcast_to(features, (row_devices, slab, width)), "row", 0, 0, tiled=True
-    ).reshape(cols, width)
+    half = row_devices // 2
+    own = features[0]
+    far = swap(own, "row", half)
     cots = exchange([cotangent[0]] * col_devices, "col")
-
-    half = row_devices // 2
-    adj, cot_block, keep, send = pl.pallas_call(
-        backward_kernel,
-        out_shape=[shape(rows, cols), shape(rows, width)] + [shape(half, slab, width)] * 2,
+    features_got = exchange([jnp.stack([own, far])] * half, "row")
+
+    adj, cot_block, *column_pairs = pl.pallas_call(
+        lambda *refs: backward_kernel(*refs, col_devices=col_devices),
+        out_shape=[shape(rows, cols), shape(rows, width)] + [shape(2, slab, width)] * half,
         in_specs=[SMEM] * 3 + [VMEM] * (1 + col_devices),
-        out_specs=[VMEM] * 4,
+        out_specs=[VMEM] * (2 + half),
         scratch_shapes=[pltpu.VMEM((cols, width), BF16)],
         compiler_params=limits,
         name="backward",
     )(me, tile_slots[0, 0], tile_counts[0], tile_values[0, 0], *cots)
-    column_chunks = pl.pallas_call(
+    column_got = exchange(column_pairs, "row")
+    column_keep, column_send = pl.pallas_call(
         pair_sum_kernel,
-        out_shape=[shape(slab, width)] * half,
-        in_specs=[SMEM, VMEM, VMEM],
-        out_specs=[VMEM] * half,
-        compiler_params=limits,
+        out_shape=[shape(slab, width, dtype=F32), shape(slab, width)],
+        in_specs=[VMEM] * half,
+        out_specs=[VMEM] * 2,
+        compiler_params=limits,
+        cost_estimate=hint(20),
         name="pair_sum",
-    )(me, keep, swap(send, "row", 1))
-    column_terms = exchange(column_chunks, "row", 2)
-
-    *row_chunks, grad = pl.pallas_call(
-        forward_kernel,
-        out_shape=[shape(slab, width)] * col_devices + [shape(width, width)],
-        in_specs=[SMEM] + [VMEM] * 3,
-        out_specs=[VMEM] * (col_devices + 1),
-        scratch_shapes=[pltpu.VMEM((rows, width), BF16)],
+    )(*column_got)
+    grad, *row_chunks = pl.pallas_call(
+        lambda *refs: forward_kernel(*refs, half=half),
+        out_shape=[shape(width, width)] + [shape(slab, width)] * col_devices,
+        in_specs=[SMEM] + [VMEM] * (2 + half),
+        out_specs=[VMEM] * (1 + col_devices),
+        scratch_shapes=[pltpu.VMEM((cols, width), BF16), pltpu.VMEM((rows, width), BF16)],
         compiler_params=limits,
         name="forward",
-    )(me, adj, column, cot_block)
+    )(me, adj, cot_block, *features_got)
+    column_terms = [column_keep, swap(column_send, "row", half)]
     row_terms = exchange(row_chunks, "col")
 
     chunk_shape = (
@@ -163,11 +175,11 @@
     grad_chunks = pl.pallas_call(
         lambda *refs: grad_sum_kernel(*refs, scale=scale),
         out_shape=shape(devices, *chunk_shape),
-        in_specs=[VMEM] + [pl.BlockSpec(memory_space=pl.ANY)] * half,
+        in_specs=[VMEM] + [pl.BlockSpec(memory_space=pl.ANY)],
         out_specs=VMEM,
         compiler_params=limits,
         name="grad_sum",
-    )(grad_terms, *column_chunks)
+    )(grad_terms, column_send)
     grad_all = lax.all_to_all(grad_chunks, ("row", "col"), 0, 0, tiled=True)
     weight_grad = grad_all.astype(F32).reshape(width, width)
 

time: 55.4 us -> 53.7 us (0.969)
  waiting for transfers between devices: 19.8 us -> 18 us
  Pallas kernels: 6.97 us -> 5.6 us
  starting transfers between devices: 23.7 us -> 24.9 us
  other arithmetic: 0.8 us -> 1.68 us
    ppermute x10 -> x14, starting transfers between devices: 9.93 us -> 17.7 us  [swap(): return lax.ppermute(array, axis, pairs)]
    all_to_all x1 -> x0, starting transfers between devices: 7.38 us -> none  [body(): lax.all_to_all(jnp.broadcast_to(features, (row_devices, slab, width)), 'r...]
    all_to_all x1 -> x0, waiting for transfers between devices: 4.16 us -> none  [body(): lax.all_to_all(jnp.broadcast_to(features, (row_devices, slab, width)), 'r...]
    ppermute x10 -> x14, waiting for transfers between devices: 8.02 us -> 9.86 us  [swap(): return lax.ppermute(array, axis, pairs)]
    broadcast_in_dim x1 -> x0, local copies, waits for them, and re-layouts: 1.77 us -> none  [body(): jnp.broadcast_to(features, (row_devices, slab, width))]
    pallas_call x3, Pallas kernels: 4.64 us -> 3.28 us  [the longest x1 1.96 us: body(): pl.pallas_call(lambda *refs: forward_kernel(*refs, half=half), out_shape=...]
    unnamed x8, local copies, waits for them, and re-layouts: 0.66 us -> 1.89 us
    another operation x0 -> x1, other arithmetic: none -> 0.88 us  [body(): features_got = exchange([jnp.stack([own, far])] * half, 'row')]
  transfers between devices with their start and end apart: 13 -> 16, of which waited for: 7 -> 5; matrix products, arithmetic and copies ran while one was open for 0% -> 0% of each run, Pallas kernels for 11% -> 9%
where the time goes in v1:
time: 53.7 us; the launch traced here: 53.4 us
  starting transfers between devices  24.9 us (46%)
  waiting for transfers between devices  18 us (34%)
  Pallas kernels  5.6 us (10%)
  local copies, waits for them, and re-layouts  1.89 us (4%)
  other arithmetic  1.68 us (3%)
  between operations  1.36 us (3%)
    ppermute x14, starting transfers between devices, swap(): return lax.ppermute(array, axis, pairs)  17.7 us
    ppermute x14, waiting for transfers between devices, swap(): return lax.ppermute(array, axis, pairs)  9.86 us
    all_to_all x1, waiting for transfers between devices, body(): lax.all_to_all(grad.reshape(devices, *chunk_shape), ('row', 'col'), 0, 0,...  8.12 us
    all_to_all x1, starting transfers between devices, body(): lax.all_to_all(grad.reshape(devices, *chunk_shape), ('row', 'col'), 0, 0,...  4.52 us
    all_to_all x1, starting transfers between devices, body(): grad_all = lax.all_to_all(grad_chunks, ('row', 'col'), 0, 0, tiled=True)  2.71 us
    pallas_call x1, Pallas kernels, body(): pl.pallas_call(lambda *refs: forward_kernel(*refs, half=half), out_shape=...  1.96 us
    unnamed x8, local copies, waits for them, and re-layouts  1.89 us
    pallas_call x2, Pallas kernels, summed_product(): pl.pallas_call(lambda *refs: product_kernel(*refs, contract=contract), ou...  1.62 us
  transfers between devices with their start and end apart: 16, of which 5 were waited for; matrix products, arithmetic and copies ran while one was open for 0% of the time, Pallas kernels for 9%

profile of v1, /device:TPU:0, one launch (start us, length us, event | category | flops | bytes accessed | tf_op | source)
XLA Modules:
  0.0 53.4 jit_solution(1526377107450477770)
XLA Ops:
  0.6 4.1 %collective-permute-start.3 = (bf16[128,256]{1,0:T(8,128)(2,1)}, bf16[128,256]{1,0:T(8,128)(2,1)S(1)}, u32[]{:S(2)}, u32[]{:S(2)}) collective-permute-start(bf16[128,256]{1,0:T(8,128)(2,1)} %bitcast.22), channel_id=1, source_target_pairs={{0,16},{4,20},{8,24},{12,28},{16,0},{20,4},{24,8},{28,12},{1,17},{... | collective-permute-start | bytes 196616 | tf_op jit(solution)/shard_map/ppermute | solution.py:115
  4.7 3.9 %collective-permute-done.3 = bf16[128,256]{1,0:T(8,128)(2,1)S(1)} collective-permute-done((bf16[128,256]{1,0:T(8,128)(2,1)}, bf16[128,256]{1,0:T(8,128)(2,1)S(1)}, u32[]{:S(2)}, u32[]{:S(2)}) %collective-permute-start.3) | collective-permute-done | bytes 65568 | tf_op jit(solution)/shard_map/ppermute | solution.py:115
  8.6 0.0 copy-start.2
  8.6 0.9 %pad_maximum_fusion.refs_3_ = bf16[2,128,256]{2,1,0:T(8,128)(2,1)S(1)} fusion(bf16[1,128,256]{2,1,0:T(8,128)(2,1)S(1)} %bitcast.24, bf16[1,128,256]{2,1,0:T(8,128)(2,1)} %param.6), kind=kLoop, calls=%fused_computation | loop fusion | flops 65536 | bytes 262144 | tf_op jit(solution)/shard_map/stack | solution.py:135
  9.5 1.8 %collective-permute-start.4 = (bf16[2,128,256]{2,1,0:T(8,128)(2,1)S(1)}, bf16[2,128,256]{2,1,0:T(8,128)(2,1)S(1)}, u32[]{:S(2)}, u32[]{:S(2)}) collective-permute-start(bf16[2,128,256]{2,1,0:T(8,128)(2,1)S(1)} %pad_maximum_fusion.refs_3_), channel_id=1, source_target_pairs={{0,4},{4,0},{8,12},{12,8},{16,20},{20,16},{24,28},{28,24},{1,5},{5... | collective-permute-start | bytes 393224 | tf_op jit(solution)/shard_map/ppermute | solution.py:115
  11.2 0.0 copy-done.2
  11.2 0.0 collective-permute-start
  11.3 1.5 %collective-permute-start.1 = (bf16[128,256]{1,0:T(8,128)(2,1)S(1)}, bf16[128,256]{1,0:T(8,128)(2,1)S(1)}, u32[]{:S(2)}, u32[]{:S(2)}) collective-permute-start(bf16[128,256]{1,0:T(8,128)(2,1)S(1)} %bitcast.17), channel_id=1, source_target_pairs={{0,2},{1,3},{2,0},{3,1},{4,6},{5,7},{6,4},{7,5},{8,10},{9,11},{10,... | collective-permute-start | bytes 196616 | tf_op jit(solution)/shard_map/ppermute | solution.py:115
  12.8 0.3 collective-permute-start.2
  13.8 0.1 pad_add_fusion.refs_0_
  13.8 0.5 collective-permute-start.5
  14.3 0.0 collective-permute-done.refs_5_
  14.3 1.3 %collective-permute-start.6 = (bf16[2,128,256]{2,1,0:T(8,128)(2,1)S(1)}, bf16[2,128,256]{2,1,0:T(8,128)(2,1)S(1)}, u32[]{:S(2)}, u32[]{:S(2)}) collective-permute-start(bf16[2,128,256]{2,1,0:T(8,128)(2,1)S(1)} %pad_maximum_fusion.refs_3_), channel_id=1, source_target_pairs={{0,12},{4,8},{8,4},{12,0},{16,28},{20,24},{24,20},{28,16},{1,13},{... | collective-permute-start | bytes 393224 | tf_op jit(solution)/shard_map/ppermute | solution.py:115
  15.7 0.1 collective-permute-done.1.refs_6_
  15.8 1.1 %collective-permute-done.2.refs_7_ = bf16[128,256]{1,0:T(8,128)(2,1)S(1)} collective-permute-done((bf16[128,256]{1,0:T(8,128)(2,1)S(1)}, bf16[128,256]{1,0:T(8,128)(2,1)S(1)}, u32[]{:S(2)}, u32[]{:S(2)}) %collective-permute-start.2) | collective-permute-done | bytes 65568 | tf_op jit(solution)/shard_map/ppermute | solution.py:115
  16.8 0.0 copy-start.3
  16.8 0.7 %copy-done.3 = s32[1,1,32]{2,1,0:T(1,128)S(1)} copy-done((s32[1,1,32]{2,1,0:T(1,128)S(1)}, s32[1,1,32]{2,1,0:T(1,128)}, u32[]{:S(2)}) %copy-start.3) | copy-done | bytes 152
  17.5 0.0 copy-start
  17.5 1.2 %copy-done = bf16[1,1,32,128,128]{4,3,2,1,0:T(8,128)(2,1)S(1)} copy-done((bf16[1,1,32,128,128]{4,3,2,1,0:T(8,128)(2,1)S(1)}, bf16[1,1,32,128,128]{4,3,2,1,0:T(8,128)(2,1)}, u32[]{:S(2)}) %copy-start) | copy-done | bytes 1048600
  18.7 1.2 %backward.1 = (bf16[512,1024]{1,0:T(8,128)(2,1)S(1)}, bf16[512,256]{1,0:T(8,128)(2,1)S(1)}, bf16[2,128,256]{2,1,0:T(8,128)(2,1)S(1)}, bf16[2,128,256]{2,1,0:T(8,...) custom-call(s32[2]{0:T(128)S(1)} %pad_add_fusion.refs_0_, s32[32]{0:T(128)S(1)} %bitcast.20, ...), custom_call_target="tpu_custom_call" | custom-call | tf_op jit(solution)/shard_map/backward/pallas_call | solution.py:137
  20.0 0.8 %collective-permute-start.10 = (bf16[2,128,256]{2,1,0:T(8,128)(2,1)S(1)}, bf16[2,128,256]{2,1,0:T(8,128)(2,1)S(1)}, u32[]{:S(2)}, u32[]{:S(2)}) collective-permute-start(bf16[2,128,256]{2,1,0:T(8,128)(2,1)S(1)} %get-tuple-element.23), channel_id=1, source_target_pairs={{0,4},{4,0},{8,12},{12,8},{16,20},{20,16},{24,28},{28,24},{1,5},{5... | collective-permute-start | bytes 393224 | tf_op jit(solution)/shard_map/ppermute | solution.py:115
  20.8 0.3 collective-permute-start.11
  21.1 0.0 collective-permute-done.4.refs_4_
  21.1 2.4 %collective-permute-start.12 = (bf16[2,128,256]{2,1,0:T(8,128)(2,1)S(1)}, bf16[2,128,256]{2,1,0:T(8,128)(2,1)S(1)}, u32[]{:S(2)}, u32[]{:S(2)}) collective-permute-start(bf16[2,128,256]{2,1,0:T(8,128)(2,1)S(1)} %get-tuple-element.25), channel_id=1, source_target_pairs={{0,12},{4,8},{8,4},{12,0},{16,28},{20,24},{24,20},{28,16},{1,13},{... | collective-permute-start | bytes 393224 | tf_op jit(solution)/shard_map/ppermute | solution.py:115
  23.5 0.0 collective-permute-done.5.refs_5_
  23.5 0.0 collective-permute-done.6.refs_6_
  23.5 2.0 %forward.1 = (bf16[256,256]{1,0:T(8,128)(2,1)}, bf16[128,256]{1,0:T(8,128)(2,1)S(1)}, bf16[128,256]{1,0:T(8,128)(2,1)S(1)}, bf16[128,256]{1,0:T(8,128)(2,1)S(1)}, bf16[128,256]{1,0:T(8,128)(2,1)S(1)}) custom-call(s32[2]{0:T(128)S(1)} %pad_add_fusion.refs_0_, bf16[512,1024]{1,0:T(8,128)(2,1)S(1)} %get-tuple-element.16.refs_1_, ...), custom_call_target="tpu_custom_call" | custom-call | tf_op jit(solution)/shard_map/forward/pallas_call | solution.py:156
  25.5 4.5 %all-to-all-start = ((bf16[32,8,256]{2,1,0:T(8,128)(2,1)}), bf16[32,8,256]{2,1,0:T(8,128)(2,1)S(1)}, u32[]{:S(2)}, u32[]{:S(2)}) async-start(bf16[32,8,256]{2,1,0:T(8,128)(2,1)} %bitcast.10), calls=%async_computation | async-start | bytes 262144 | tf_op jit(solution)/shard_map/all_to_all | solution.py:171
  30.0 0.0 collective-permute-done.10.refs_1_
  30.0 0.0 collective-permute-done.11.refs_2_
  30.1 0.0 collective-permute-done.12.refs_3_
  30.1 0.1 pair_sum.1
  30.1 8.1 %all-to-all-done.refs_0_ = bf16[32,8,256]{2,1,0:T(8,128)(2,1)S(1)} async-done(((bf16[32,8,256]{2,1,0:T(8,128)(2,1)}), bf16[32,8,256]{2,1,0:T(8,128)(2,1)S(1)}, u32[]{:S(2)}, u32[]{:S(2)}) %all-to-all-start) | async-done | bytes 131104 | tf_op jit(solution)/shard_map/all_to_all | solution.py:171
  38.3 0.7 %grad_sum.1 = bf16[32,8,256]{2,1,0:T(8,128)(2,1)} custom-call(bf16[32,8,256]{2,1,0:T(8,128)(2,1)S(1)} %all-to-all-done.refs_0_, bf16[128,256]{1,0:T(8,128)(2,1)S(1)} %get-tuple-element.27.refs_1_), custom_call_target="tpu_custom_call" | custom-call | tf_op jit(solution)/shard_map/grad_sum/pallas_call | solution.py:175
  39.0 2.7 %all-to-all-start.1 = ((bf16[32,8,256]{2,1,0:T(8,128)(2,1)}), bf16[32,8,256]{2,1,0:T(8,128)(2,1)S(1)}, u32[]{:S(2)}, u32[]{:S(2)}) async-start(bf16[32,8,256]{2,1,0:T(8,128)(2,1)} %grad_sum.1), calls=%async_computation.1 | async-start | bytes 262144 | tf_op jit(solution)/shard_map/all_to_all | solution.py:183
  41.7 2.7 %collective-permute-start.13 = (bf16[128,256]{1,0:T(8,128)(2,1)S(1)}, bf16[128,256]{1,0:T(8,128)(2,1)S(1)}, u32[]{:S(2)}, u32[]{:S(2)}) collective-permute-start(bf16[128,256]{1,0:T(8,128)(2,1)S(1)} %get-tuple-element.27.refs_1_), channel_id=1, source_target_pairs={{0,16},{4,20},{8,24},{12,28},{16,0},{20,4},{24,8},{28,12},{1,17},{... | collective-permute-start | bytes 196616 | tf_op jit(solution)/shard_map/ppermute | solution.py:115
  44.4 0.0 collective-permute-start.7
  44.4 1.5 %collective-permute-start.8 = (bf16[128,256]{1,0:T(8,128)(2,1)S(1)}, bf16[128,256]{1,0:T(8,128)(2,1)S(1)}, u32[]{:S(2)}, u32[]{:S(2)}) collective-permute-start(bf16[128,256]{1,0:T(8,128)(2,1)S(1)} %get-tuple-element.20), channel_id=1, source_target_pairs={{0,2},{1,3},{2,0},{3,1},{4,6},{5,7},{6,4},{7,5},{8,10},{9,11},{10,... | collective-permute-start | bytes 196616 | tf_op jit(solution)/shard_map/ppermute | solution.py:115
  45.9 0.4 collective-permute-start.9
  46.3 4.8 %collective-permute-done.13.refs_2_ = bf16[128,256]{1,0:T(8,128)(2,1)S(1)} collective-permute-done((bf16[128,256]{1,0:T(8,128)(2,1)S(1)}, bf16[128,256]{1,0:T(8,128)(2,1)S(1)}, u32[]{:S(2)}, u32[]{:S(2)}) %collective-permute-start.13) | collective-permute-done | bytes 65568 | tf_op jit(solution)/shard_map/ppermute | solution.py:115
  51.0 0.0 copy-done.1
  51.0 0.8 %feature_grad.1 = bf16[128,256]{1,0:T(8,128)(2,1)} custom-call(bf16[256,256]{1,0:T(8,128)(2,1)S(1)} %copy-done.1, f32[128,256]{1,0:T(8,128)S(1)} %get-tuple-element.26.refs_1_, bf16[128,256]{1,0:T(8,128)(2,1)S(1)} %collective-permute-done.13.refs_2_), custom_call_target="tpu_custom_call" | custom-call | tf_op jit(solution)/shard_map/feature_grad/pallas_call | solution.py:103
  51.9 0.0 collective-permute-done.7.refs_2_
  51.9 0.0 collective-permute-done.8.refs_3_
  51.9 0.0 collective-permute-done.9.refs_4_
  51.9 0.8 %layer_out.1 = bf16[128,256]{1,0:T(8,128)(2,1)} custom-call(bf16[256,256]{1,0:T(8,128)(2,1)S(1)} %copy-done.1, bf16[128,256]{1,0:T(8,128)(2,1)S(1)} %get-tuple-element.18.refs_1_, bf16[128,256]{1,0:T(8,128)(2,1)S(1)} %collective-permute-done.7.refs_2_, bf16[128,256]{1,0:T(8,128)(2,1)S(1)} %collective-permute-done.8.refs_3_, ...), custom_call_target="tpu_custom_call" | custom-call | tf_op jit(solution)/shard_map/layer_out/pallas_call | solution.py:103
  52.7 0.0 all-to-all-done.1
  52.7 0.7 %bitcast_convert_fusion = f32[256,256]{1,0:T(8,128)} fusion(bf16[32,8,256]{2,1,0:T(8,128)(2,1)S(1)} %all-to-all-done.1), kind=kLoop, calls=%fused_computation.1 | loop fusion | flops 65536 | bytes 393216 | tf_op jit(solution)/shard_map/reshape | solution.py:184
  (1 shorter events, 0.0 us)
Async XLA Ops:
  0.6 8.0 %collective-permute-start.3 = (bf16[128,256]{1,0:T(8,128)(2,1)}, bf16[128,256]{1,0:T(8,128)(2,1)S(1)}, u32[]{:S(2)}, u32[]{:S(2)}) collective-permute-start(bf16[128,256]{1,0:T(8,128)(2,1)} %bitcast.22), channel_id=1, source_target_pairs={{0,16},{4,20},{8,24},{12,28},{16,0},{20,4},{24,8},{28,12},{1,17},{... | collective-permute-start | bytes 196616 | tf_op jit(solution)/shard_map/ppermute | solution.py:115
  8.6 2.7 %copy-start.2 = (bf16[1,128,256]{2,1,0:T(8,128)(2,1)S(1)}, bf16[1,128,256]{2,1,0:T(8,128)(2,1)}, u32[]{:S(2)}) copy-start(bf16[1,128,256]{2,1,0:T(8,128)(2,1)} %param.11) | copy-start | bytes 196612
  9.5 11.6 %collective-permute-start.4 = (bf16[2,128,256]{2,1,0:T(8,128)(2,1)S(1)}, bf16[2,128,256]{2,1,0:T(8,128)(2,1)S(1)}, u32[]{:S(2)}, u32[]{:S(2)}) collective-permute-start(bf16[2,128,256]{2,1,0:T(8,128)(2,1)S(1)} %pad_maximum_fusion.refs_3_), channel_id=1, source_target_pairs={{0,4},{4,0},{8,12},{12,8},{16,20},{20,16},{24,28},{28,24},{1,5},{5... | collective-permute-start | bytes 393224 | tf_op jit(solution)/shard_map/ppermute | solution.py:115
  11.2 3.1 %collective-permute-start = (bf16[128,256]{1,0:T(8,128)(2,1)S(1)}, bf16[128,256]{1,0:T(8,128)(2,1)S(1)}, u32[]{:S(2)}, u32[]{:S(2)}) collective-permute-start(bf16[128,256]{1,0:T(8,128)(2,1)S(1)} %bitcast.16), channel_id=1, source_target_pairs={{0,1},{1,0},{2,3},{3,2},{4,5},{5,4},{6,7},{7,6},{8,9},{9,8},{10,11... | collective-permute-start | bytes 196616 | tf_op jit(solution)/shard_map/ppermute | solution.py:115
  11.3 4.5 %collective-permute-start.1 = (bf16[128,256]{1,0:T(8,128)(2,1)S(1)}, bf16[128,256]{1,0:T(8,128)(2,1)S(1)}, u32[]{:S(2)}, u32[]{:S(2)}) collective-permute-start(bf16[128,256]{1,0:T(8,128)(2,1)S(1)} %bitcast.17), channel_id=1, source_target_pairs={{0,2},{1,3},{2,0},{3,1},{4,6},{5,7},{6,4},{7,5},{8,10},{9,11},{10,... | collective-permute-start | bytes 196616 | tf_op jit(solution)/shard_map/ppermute | solution.py:115
  12.8 4.1 %collective-permute-start.2 = (bf16[128,256]{1,0:T(8,128)(2,1)S(1)}, bf16[128,256]{1,0:T(8,128)(2,1)S(1)}, u32[]{:S(2)}, u32[]{:S(2)}) collective-permute-start(bf16[128,256]{1,0:T(8,128)(2,1)S(1)} %bitcast.18), channel_id=1, source_target_pairs={{0,3},{1,2},{2,1},{3,0},{4,7},{5,6},{6,5},{7,4},{8,11},{9,10},{10,... | collective-permute-start | bytes 196616 | tf_op jit(solution)/shard_map/ppermute | solution.py:115
  13.8 9.7 %collective-permute-start.5 = (bf16[2,128,256]{2,1,0:T(8,128)(2,1)S(1)}, bf16[2,128,256]{2,1,0:T(8,128)(2,1)S(1)}, u32[]{:S(2)}, u32[]{:S(2)}) collective-permute-start(bf16[2,128,256]{2,1,0:T(8,128)(2,1)S(1)} %pad_maximum_fusion.refs_3_), channel_id=1, source_target_pairs={{0,8},{4,12},{8,0},{12,4},{16,24},{20,28},{24,16},{28,20},{1,9},{5... | collective-permute-start | bytes 393224 | tf_op jit(solution)/shard_map/ppermute | solution.py:115
  14.3 9.2 %collective-permute-start.6 = (bf16[2,128,256]{2,1,0:T(8,128)(2,1)S(1)}, bf16[2,128,256]{2,1,0:T(8,128)(2,1)S(1)}, u32[]{:S(2)}, u32[]{:S(2)}) collective-permute-start(bf16[2,128,256]{2,1,0:T(8,128)(2,1)S(1)} %pad_maximum_fusion.refs_3_), channel_id=1, source_target_pairs={{0,12},{4,8},{8,4},{12,0},{16,28},{20,24},{24,20},{28,16},{1,13},{... | collective-permute-start | bytes 393224 | tf_op jit(solution)/shard_map/ppermute | solution.py:115
  16.8 0.7 %copy-start.3 = (s32[1,1,32]{2,1,0:T(1,128)S(1)}, s32[1,1,32]{2,1,0:T(1,128)}, u32[]{:S(2)}) copy-start(s32[1,1,32]{2,1,0:T(1,128)} %param.9) | copy-start | bytes 388
  17.5 1.2 %copy-start = (bf16[1,1,32,128,128]{4,3,2,1,0:T(8,128)(2,1)S(1)}, bf16[1,1,32,128,128]{4,3,2,1,0:T(8,128)(2,1)}, u32[]{:S(2)}) copy-start(bf16[1,1,32,128,128]{4,3,2,1,0:T(8,128)(2,1)} %param.8) | copy-start | bytes 3145732
  20.0 10.1 %collective-permute-start.10 = (bf16[2,128,256]{2,1,0:T(8,128)(2,1)S(1)}, bf16[2,128,256]{2,1,0:T(8,128)(2,1)S(1)}, u32[]{:S(2)}, u32[]{:S(2)}) collective-permute-start(bf16[2,128,256]{2,1,0:T(8,128)(2,1)S(1)} %get-tuple-element.23), channel_id=1, source_target_pairs={{0,4},{4,0},{8,12},{12,8},{16,20},{20,16},{24,28},{28,24},{1,5},{5... | collective-permute-start | bytes 393224 | tf_op jit(solution)/shard_map/ppermute | solution.py:115
  20.8 9.3 %collective-permute-start.11 = (bf16[2,128,256]{2,1,0:T(8,128)(2,1)S(1)}, bf16[2,128,256]{2,1,0:T(8,128)(2,1)S(1)}, u32[]{:S(2)}, u32[]{:S(2)}) collective-permute-start(bf16[2,128,256]{2,1,0:T(8,128)(2,1)S(1)} %get-tuple-element.24), channel_id=1, source_target_pairs={{0,8},{4,12},{8,0},{12,4},{16,24},{20,28},{24,16},{28,20},{1,9},{5... | collective-permute-start | bytes 393224 | tf_op jit(solution)/shard_map/ppermute | solution.py:115
  21.1 9.0 %collective-permute-start.12 = (bf16[2,128,256]{2,1,0:T(8,128)(2,1)S(1)}, bf16[2,128,256]{2,1,0:T(8,128)(2,1)S(1)}, u32[]{:S(2)}, u32[]{:S(2)}) collective-permute-start(bf16[2,128,256]{2,1,0:T(8,128)(2,1)S(1)} %get-tuple-element.25), channel_id=1, source_target_pairs={{0,12},{4,8},{8,4},{12,0},{16,28},{20,24},{24,20},{28,16},{1,13},{... | collective-permute-start | bytes 393224 | tf_op jit(solution)/shard_map/ppermute | solution.py:115
  25.5 12.8 %all-to-all-start = ((bf16[32,8,256]{2,1,0:T(8,128)(2,1)}), bf16[32,8,256]{2,1,0:T(8,128)(2,1)S(1)}, u32[]{:S(2)}, u32[]{:S(2)}) async-start(bf16[32,8,256]{2,1,0:T(8,128)(2,1)} %bitcast.10), calls=%async_computation | async-start | bytes 262144 | tf_op jit(solution)/shard_map/all_to_all | solution.py:171
  39.0 12.1 %copy-start.1 = (bf16[256,256]{1,0:T(8,128)(2,1)S(1)}, bf16[256,256]{1,0:T(8,128)(2,1)}, u32[]{:S(2)}) copy-start(bf16[256,256]{1,0:T(8,128)(2,1)} %refs_0_.3) | copy-start | bytes 393220
  39.0 13.7 %all-to-all-start.1 = ((bf16[32,8,256]{2,1,0:T(8,128)(2,1)}), bf16[32,8,256]{2,1,0:T(8,128)(2,1)S(1)}, u32[]{:S(2)}, u32[]{:S(2)}) async-start(bf16[32,8,256]{2,1,0:T(8,128)(2,1)} %grad_sum.1), calls=%async_computation.1 | async-start | bytes 262144 | tf_op jit(solution)/shard_map/all_to_all | solution.py:183
  41.7 9.4 %collective-permute-start.13 = (bf16[128,256]{1,0:T(8,128)(2,1)S(1)}, bf16[128,256]{1,0:T(8,128)(2,1)S(1)}, u32[]{:S(2)}, u32[]{:S(2)}) collective-permute-start(bf16[128,256]{1,0:T(8,128)(2,1)S(1)} %get-tuple-element.27.refs_1_), channel_id=1, source_target_pairs={{0,16},{4,20},{8,24},{12,28},{16,0},{20,4},{24,8},{28,12},{1,17},{... | collective-permute-start | bytes 196616 | tf_op jit(solution)/shard_map/ppermute | solution.py:115
  44.4 7.5 %collective-permute-start.7 = (bf16[128,256]{1,0:T(8,128)(2,1)S(1)}, bf16[128,256]{1,0:T(8,128)(2,1)S(1)}, u32[]{:S(2)}, u32[]{:S(2)}) collective-permute-start(bf16[128,256]{1,0:T(8,128)(2,1)S(1)} %get-tuple-element.19), channel_id=1, source_target_pairs={{0,1},{1,0},{2,3},{3,2},{4,5},{5,4},{6,7},{7,6},{8,9},{9,8},{10,11... | collective-permute-start | bytes 196616 | tf_op jit(solution)/shard_map/ppermute | solution.py:115
  44.4 7.5 %collective-permute-start.8 = (bf16[128,256]{1,0:T(8,128)(2,1)S(1)}, bf16[128,256]{1,0:T(8,128)(2,1)S(1)}, u32[]{:S(2)}, u32[]{:S(2)}) collective-permute-start(bf16[128,256]{1,0:T(8,128)(2,1)S(1)} %get-tuple-element.20), channel_id=1, source_target_pairs={{0,2},{1,3},{2,0},{3,1},{4,6},{5,7},{6,4},{7,5},{8,10},{9,11},{10,... | collective-permute-start | bytes 196616 | tf_op jit(solution)/shard_map/ppermute | solution.py:115
  45.9 6.0 %collective-permute-start.9 = (bf16[128,256]{1,0:T(8,128)(2,1)S(1)}, bf16[128,256]{1,0:T(8,128)(2,1)S(1)}, u32[]{:S(2)}, u32[]{:S(2)}) collective-permute-start(bf16[128,256]{1,0:T(8,128)(2,1)S(1)} %get-tuple-element.21), channel_id=1, source_target_pairs={{0,3},{1,2},{2,1},{3,0},{4,7},{5,6},{6,5},{7,4},{8,11},{9,10},{10,... | collective-permute-start | bytes 196616 | tf_op jit(solution)/shard_map/ppermute | solution.py:115
